TPU v7x, 32 devices: a whole 2x2x4 slice. The times are simulated.
32 devices in a mesh: rep: 4 (over z), shard: 8 (over y, x, core).
Axes of the slice: x: 2, y: 2, z: 4, core: 2. Of those that a mesh axis runs over, the one named last changes fastest.
Arguments:
- trained_sq: float32 [4, 4, 768, 768], P('rep', None, 'shard'), may hold values from -6 to 6
- trained_up: float32 [4, 768, 3072], P('rep', 'shard'), may hold values from -6 to 6
- trained_down: float32 [4, 3072, 768], P('rep', 'shard'), may hold values from -6 to 6
- trained_ln: float32 [4, 4, 768], P('rep', None, 'shard'), may hold values from -6 to 6
- start_sq: float32 [4, 768, 768], P(None, 'shard'), may hold values from -6 to 6
- start_up: float32 [768, 3072], P('shard'), may hold values from -6 to 6
- start_down: float32 [3072, 768], P('shard'), may hold values from -6 to 6
- start_ln: float32 [4, 768], P(None, 'shard'), may hold values from -6 to 6
- resid_sq: float32 [4, 4, 768, 768], P('rep', None, 'shard'), may hold values from -4 to 4
- resid_up: float32 [4, 768, 3072], P('rep', 'shard'), may hold values from -4 to 4
- resid_down: float32 [4, 3072, 768], P('rep', 'shard'), may hold values from -4 to 4
- mom_sq: float32 [4, 768, 768], P(None, 'shard'), may hold values from -3 to 3
- mom_up: float32 [768, 3072], P('shard'), may hold values from -3 to 3
- mom_down: float32 [3072, 768], P('shard'), may hold values from -3 to 3
- mom_ln: float32 [4, 768], P(None, 'shard'), may hold values from -3 to 3
- basis_sq: float32 [4, 768, 64], replicated, may hold values from -0.21875 to 0.21875
- basis_up: float32 [3072, 64], replicated, may hold values from -0.109375 to 0.109375
- basis_down: float32 [768, 64], replicated, may hold values from -0.21875 to 0.21875
Outputs:
- new_resid_sq: float32 [4, 4, 768, 768], P('rep', None, 'shard')
- new_resid_up: float32 [4, 768, 3072], P('rep', 'shard')
- new_resid_down: float32 [4, 3072, 768], P('rep', 'shard')
- new_mom_sq: float32 [4, 768, 768], P(None, 'shard')
- new_mom_up: float32 [768, 3072], P('shard')
- new_mom_down: float32 [3072, 768], P('shard')
- new_mom_ln: float32 [4, 768], P(None, 'shard')
- weights_sq: bfloat16 [4, 768, 768], replicated
- weights_up: bfloat16 [768, 3072], replicated
- weights_down: bfloat16 [3072, 768], replicated
- weights_ln: bfloat16 [4, 768], replicated
All inputs are finite; a program needn't handle non-finite values.
Results may differ from a plain program's by a relative error of at most 0.001.
Values may be sent and summed in bfloat16 or wider, within the bound.
A program may use at most 128 MiB of HBM per device.

v0:
```python
import jax
import jax.numpy as jnp
from jax import lax
from jax.sharding import PartitionSpec as P

moment_coef = 0.9
outer_rate = 0.7


def advance(start, moment, outer):
    new_moment = moment_coef * moment + outer
    weights = (start - outer_rate * (outer + moment_coef * new_moment)).astype(jnp.bfloat16)
    return (new_moment, weights)


def on_device(
    trained_sq,
    trained_up,
    trained_down,
    trained_ln,
    start_sq,
    start_up,
    start_down,
    start_ln,
    resid_sq,
    resid_up,
    resid_down,
    mom_sq,
    mom_up,
    mom_down,
    mom_ln,
    basis_sq,
    basis_up,
    basis_down,
):
    highest = lax.Precision.HIGHEST
    groups = lax.axis_size("rep")
    delta_sq = start_sq - trained_sq[0] + resid_sq[0]
    factor_sq = jnp.einsum("mrd,mdk->mrk", delta_sq, basis_sq, precision=highest)
    new_resid_sq = delta_sq - jnp.einsum("mrk,mdk->mrd", factor_sq, basis_sq, precision=highest)
    delta_up = start_up - trained_up[0] + resid_up[0]
    factor_up = jnp.dot(delta_up, basis_up, precision=highest, preferred_element_type=jnp.float32)
    new_resid_up = delta_up - jnp.einsum("rk,fk->rf", factor_up, basis_up, precision=highest)
    delta_down = start_down - trained_down[0] + resid_down[0]
    factor_down = jnp.dot(
        delta_down, basis_down, precision=highest, preferred_element_type=jnp.float32
    )
    new_resid_down = delta_down - jnp.einsum(
        "rk,dk->rd", factor_down, basis_down, precision=highest
    )
    norm_delta = start_ln - trained_ln[0]
    summed = lax.psum((factor_sq, factor_up, factor_down, norm_delta), "rep")
    mean_sq = summed[0] / groups
    mean_up = summed[1] / groups
    mean_down = summed[2] / groups
    mean_ln = summed[3] / groups
    new_mom_ln, norm_weights = advance(start_ln, mom_ln, mean_ln)
    outer_sq = jnp.einsum("mrk,mdk->mrd", mean_sq, basis_sq, precision=highest)
    outer_up = jnp.einsum("rk,fk->rf", mean_up, basis_up, precision=highest)
    outer_down = jnp.einsum("rk,dk->rd", mean_down, basis_down, precision=highest)
    new_mom_sq, owned_sq = advance(start_sq, mom_sq, outer_sq)
    new_mom_up, owned_up = advance(start_up, mom_up, outer_up)
    new_mom_down, owned_down = advance(start_down, mom_down, outer_down)
    weights_sq, weights_up, weights_down, weights_ln = (
        lax.all_gather(owned_sq, "shard", axis=1, tiled=True),
        lax.all_gather(owned_up, "shard", axis=0, tiled=True),
        lax.all_gather(owned_down, "shard", axis=0, tiled=True),
        lax.all_gather(norm_weights, "shard", axis=1, tiled=True),
    )
    return (
        new_resid_sq[None],
        new_resid_up[None],
        new_resid_down[None],
        new_mom_sq,
        new_mom_up,
        new_mom_down,
        new_mom_ln,
        weights_sq,
        weights_up,
        weights_down,
        weights_ln,
    )


def solution(mesh):
    placed = (
        P("rep", None, "shard", None),
        P("rep", "shard", None),
        P("rep", "shard", None),
        P("rep", None, "shard"),
        P(None, "shard", None),
        P("shard", None),
        P("shard", None),
        P(None, "shard"),
        P("rep", None, "shard", None),
        P("rep", "shard", None),
        P("rep", "shard", None),
        P(None, "shard", None),
        P("shard", None),
        P("shard", None),
        P(None, "shard"),
        P(),
        P(),
        P(),
    )
    return jax.shard_map(
        on_device,
        mesh=mesh,
        in_specs=placed,
        out_specs=(
            P("rep", None, "shard", None),
            P("rep", "shard", None),
            P("rep", "shard", None),
            P(None, "shard", None),
            P("shard", None),
            P("shard", None),
            P(None, "shard"),
            P(),
            P(),
            P(),
            P(),
        ),
        check_vma=False,
    )
```

profile of v0, /device:TPU:0, one launch (start us, length us, event | category | flops | bytes accessed | tf_op | source)
XLA Modules:
  0.0 189.1 jit_solution(14248313189104783619)
XLA Ops:
  8.0 0.0 copy-start
  8.1 1.1 copy-done
  9.2 3.6 %fusion.16 = f32[4,96,64]{1,2,0:T(8,128)S(1)} fusion(f32[4,768,64]{1,2,0:T(8,128)S(1)} %copy-done, f32[1,4,96,768]{3,2,1,0:T(8,128)} %param.26, f32[4,96,768]{2,1,0:T(8,128)} %param.22, f32[1,4,96,768]{3,2,1,0:T(8,128)} %param.18), kind=kOutput, calls=%fused_computation.34 | convolution fusion | flops 227082240 | bytes 4423680 | tf_op jit(solution)/shard_map/mrd,mdk->mrk/dot_general | solution.py:39
  12.8 0.0 copy-start.10
  12.9 2.4 %fusion.2 = f32[1,4,96,768]{3,2,1,0:T(8,128)} fusion(f32[4,96,64]{1,2,0:T(8,128)S(1)} %fusion.16, f32[4,768,64]{1,2,0:T(8,128)S(1)} %copy-done, f32[1,4,96,768]{3,2,1,0:T(8,128)S(1)} %copy-done.7, f32[4,96,768]{2,1,0:T(8,128)S(1)} %copy-done.1, f32[1,4,96,768]{3,2,1,0:T(8,128)S(1)} %copy-done.8), kind=kOutput, calls=%fused_computation.5 | convolution fusion | flops 227377152 | bytes 5603328 | tf_op jit(solution)/shard_map/mrk,mdk->mrd/dot_general | solution.py:40
  15.2 2.0 %fusion.18 = f32[384,64]{0,1:T(8,128)} fusion(f32[768,64]{0,1:T(8,128)S(1)} %copy-done.9, f32[1,384,768]{2,1,0:T(8,128)S(1)} %copy-done.5, f32[384,768]{1,0:T(8,128)S(1)} %copy-done.2, f32[1,384,768]{2,1,0:T(8,128)S(1)} %copy-done.6), kind=kOutput, calls=%fused_computation.36 | convolution fusion | flops 227082240 | bytes 3833856 | tf_op jit(solution)/shard_map/dot_general | solution.py:45
  17.2 3.9 %fusion.1 = f32[1,384,768]{2,1,0:T(8,128)} fusion(f32[384,64]{0,1:T(8,128)} %fusion.18, f32[768,64]{0,1:T(8,128)S(1)} %copy-done.9, f32[1,384,768]{2,1,0:T(8,128)} %param.28, f32[384,768]{1,0:T(8,128)S(1)} %copy-done.2, f32[1,384,768]{2,1,0:T(8,128)} %param.20), kind=kOutput, calls=%fused_computation.3 | convolution fusion | flops 227377152 | bytes 5013504 | tf_op jit(solution)/shard_map/rk,dk->rd/dot_general | solution.py:48
  21.1 0.7 all-reduce.4.cloned.1.call-update
  21.8 0.0 all-gather.7.cloned.1.call-start
  21.9 3.3 %fusion.17 = f32[96,64]{0,1:T(8,128)S(1)} fusion(f32[3072,64]{0,1:T(8,128)} %param.34, f32[1,96,3072]{2,1,0:T(8,128)} %param.27, f32[96,3072]{1,0:T(8,128)} %param.23, f32[1,96,3072]{2,1,0:T(8,128)} %param.19), kind=kOutput, calls=%fused_computation.35 | convolution fusion | flops 227082240 | bytes 4349952 | tf_op jit(solution)/shard_map/dot_general | solution.py:42
  25.2 22.1 %all-reduce = (f32[96,64]{0,1:T(8,128)S(1)}, f32[4,96]{1,0:T(4,128)S(1)}) all-reduce(f32[96,64]{0,1:T(8,128)S(1)} %fusion.17, f32[4,96]{1,0:T(4,128)S(1)} %bitcast_subtract_fusion.3), channel_id=1, replica_groups=mesh['rep'=4,'shard'=8] {'rep'}, use_global_device_ids=true, to_apply=%region_1.0 | all-reduce | flops 6528 | bytes 52224 | tf_op jit(solution)/shard_map/psum | solution.py:52
  47.3 4.4 %subtract_convert_fusion.1 = (bf16[96,3072]{1,0:T(8,128)(2,1)}, f32[96,3072]{1,0:T(8,128)}) fusion(f32[96,3072]{1,0:T(8,128)} %param.23, f32[96,3072]{1,0:T(8,128)} %param.30, f32[3072,64]{0,1:T(8,128)} %param.34, f32[96,64]{0,1:T(8,128)S(1)} %get-tuple-element.11), kind=kOutput, calls=%fused_computation.13 | convolution fusion | flops 228562944 | bytes 4939776 | tf_op jit(solution)/shard_map/rk,fk->rf/dot_general | solution.py:59
  51.8 0.0 all-gather.7.cloned.1.call-update
  51.8 0.0 all-gather.5.cloned.1.call-start
  51.8 11.5 %all-reduce.4.cloned.1.call-done = (f32[4,96,64]{1,2,0:T(8,128)}, f32[384,64]{0,1:T(8,128)}) async-done(((f32[4,96,64]{1,2,0:T(8,128)}, f32[384,64]{0,1:T(8,128)}), (f32[4,96,64]{1,2,0:T(8,128)}, f32[384,64]{0,1:T(8,128)})) %all-reduce.4.cloned.1.call-update) | async-done | bytes 196624 | tf_op jit(solution)/shard_map/psum | solution.py:52
  63.3 3.9 %subtract_convert_fusion.2 = (bf16[4,96,768]{2,1,0:T(8,128)(2,1)}, f32[4,96,768]{2,1,0:T(8,128)}) fusion(f32[4,96,768]{2,1,0:T(8,128)S(1)} %copy-done.1, f32[4,96,768]{2,1,0:T(8,128)} %param.29, f32[4,768,64]{1,2,0:T(8,128)S(1)} %copy-done, f32[4,96,64]{1,2,0:T(8,128)} %get-tuple-element.13), kind=kOutput, calls=%fused_computation.14 | convolution fusion | flops 228581376 | bytes 5013504 | tf_op jit(solution)/shard_map/mrk,mdk->mrd/dot_general | solution.py:58
  67.2 0.0 all-gather.5.cloned.1.call-update
  67.3 0.0 all-gather.9.cloned.1.call-start
  67.4 3.9 %subtract_convert_fusion = (bf16[384,768]{1,0:T(8,128)(2,1)}, f32[384,768]{1,0:T(8,128)}) fusion(f32[384,768]{1,0:T(8,128)S(1)} %copy-done.2, f32[384,768]{1,0:T(8,128)} %param.31, f32[768,64]{0,1:T(8,128)S(1)} %copy-done.9, f32[384,64]{0,1:T(8,128)S(1)} %copy-done.11), kind=kOutput, calls=%fused_computation.12 | convolution fusion | flops 228581376 | bytes 4423680 | tf_op jit(solution)/shard_map/rk,dk->rd/dot_general | solution.py:60
  71.2 0.0 all-gather.9.cloned.1.call-update
  71.3 0.6 fusion.12
  71.8 8.8 %all-gather = bf16[8,96,4]{1,2,0:T(4,128)(2,1)S(1)} all-gather(bf16[1,96,4]{1,2,0:T(4,128)(2,1)S(1)} %get-tuple-element.15), channel_id=1, replica_groups=mesh['rep'=4,'shard'=8] {'shard'}, dimensions={0}, use_global_device_ids=true | all-gather | bytes 6912 | tf_op jit(solution)/shard_map/all_gather | solution.py:68
  80.7 0.7 reshape.23
  81.4 4.1 %fusion = f32[1,96,3072]{2,1,0:T(8,128)} fusion(f32[96,64]{0,1:T(8,128)S(1)} %fusion.17, f32[3072,64]{0,1:T(8,128)} %param.34, f32[1,96,3072]{2,1,0:T(8,128)} %param.27, f32[96,3072]{1,0:T(8,128)S(1)} %copy-done.3, f32[1,96,3072]{2,1,0:T(8,128)} %param.19), kind=kOutput, calls=%fused_computation.1 | convolution fusion | flops 227377152 | bytes 5529600 | tf_op jit(solution)/shard_map/rk,fk->rf/dot_general | solution.py:43
  85.5 2.6 %all-gather.7.cloned.1.call-done = bf16[768,3072]{1,0:T(8,128)(2,1)} async-done(((bf16[96,3072]{1,0:T(8,128)(2,1)}), bf16[768,3072]{1,0:T(8,128)(2,1)}) %all-gather.7.cloned.1.call-update) | async-done | bytes 4718608 | tf_op jit(solution)/shard_map/all_gather | solution.py:66
  88.1 41.3 %all-gather.5.cloned.1.call-done = bf16[4,768,768]{2,1,0:T(8,128)(2,1)} async-done(((bf16[4,96,768]{2,1,0:T(8,128)(2,1)}), bf16[4,768,768]{2,1,0:T(8,128)(2,1)}) %all-gather.5.cloned.1.call-update) | async-done | bytes 4718608 | tf_op jit(solution)/shard_map/all_gather | solution.py:65
  129.4 41.3 %all-gather.9.cloned.1.call-done = bf16[3072,768]{1,0:T(8,128)(2,1)} async-done(((bf16[384,768]{1,0:T(8,128)(2,1)}), bf16[3072,768]{1,0:T(8,128)(2,1)}) %all-gather.9.cloned.1.call-update) | async-done | bytes 4718608 | tf_op jit(solution)/shard_map/all_gather | solution.py:67
  170.7 5.2 %copy.36 = bf16[4,768,768]{2,1,0:T(8,128)(2,1)} copy(bf16[4,768,768]{2,1,0:T(8,128)(2,1)} %all-gather.5.cloned.1.call-done) | data formatting | bytes 9437184
  175.9 2.4 %copy.37 = bf16[768,3072]{1,0:T(8,128)(2,1)} copy(bf16[768,3072]{1,0:T(8,128)(2,1)S(1)} %copy-done.4) | data formatting | bytes 9437184
  178.3 0.5 slice-done
  178.7 0.5 slice-done.1
  179.3 2.2 %copy.38 = bf16[3072,768]{1,0:T(8,128)(2,1)} copy(bf16[3072,768]{1,0:T(8,128)(2,1)S(1)} %bitcast.64) | data formatting | bytes 9437184
  (33 shorter events, 0.1 us)
Async XLA Ops:
  8.0 1.1 copy-start
  8.0 4.7 %copy-start.8 = (f32[1,4,96,768]{3,2,1,0:T(8,128)S(1)}, f32[1,4,96,768]{3,2,1,0:T(8,128)}, u32[]{:S(2)}) copy-start(f32[1,4,96,768]{3,2,1,0:T(8,128)} %param.18) | copy-start | bytes 3538948
  8.0 4.7 %copy-start.1 = (f32[4,96,768]{2,1,0:T(8,128)S(1)}, f32[4,96,768]{2,1,0:T(8,128)}, u32[]{:S(2)}) copy-start(f32[4,96,768]{2,1,0:T(8,128)} %param.22) | copy-start | bytes 3538948
  8.0 4.7 %copy-start.7 = (f32[1,4,96,768]{3,2,1,0:T(8,128)S(1)}, f32[1,4,96,768]{3,2,1,0:T(8,128)}, u32[]{:S(2)}) copy-start(f32[1,4,96,768]{3,2,1,0:T(8,128)} %param.26) | copy-start | bytes 3538948
  12.8 2.4 %copy-start.10 = (f32[4,96,64]{1,2,0:T(8,128)}, f32[4,96,64]{1,2,0:T(8,128)S(1)}, u32[]{:S(2)}) copy-start(f32[4,96,64]{1,2,0:T(8,128)S(1)} %fusion.16) | copy-start | bytes 294916
  12.8 2.4 %copy-start.2 = (f32[384,768]{1,0:T(8,128)S(1)}, f32[384,768]{1,0:T(8,128)}, u32[]{:S(2)}) copy-start(f32[384,768]{1,0:T(8,128)} %param.24) | copy-start | bytes 3538948
  12.8 2.4 %copy-start.5 = (f32[1,384,768]{2,1,0:T(8,128)S(1)}, f32[1,384,768]{2,1,0:T(8,128)}, u32[]{:S(2)}) copy-start(f32[1,384,768]{2,1,0:T(8,128)} %param.28) | copy-start | bytes 3538948
  12.8 2.4 %copy-start.6 = (f32[1,384,768]{2,1,0:T(8,128)S(1)}, f32[1,384,768]{2,1,0:T(8,128)}, u32[]{:S(2)}) copy-start(f32[1,384,768]{2,1,0:T(8,128)} %param.20) | copy-start | bytes 3538948
  12.8 2.4 %copy-start.9 = (f32[768,64]{0,1:T(8,128)S(1)}, f32[768,64]{0,1:T(8,128)}, u32[]{:S(2)}) copy-start(f32[768,64]{0,1:T(8,128)} %param.35) | copy-start | bytes 589828
  17.2 4.7 %copy-start.12 = (f32[4,96]{1,0:T(4,128)S(1)}, f32[4,96]{1,0:T(4,128)}, u32[]{:S(2)}) copy-start(f32[4,96]{1,0:T(4,128)} %param.25) | copy-start | bytes 4612
  17.2 4.7 %copy-start.13 = (f32[1,4,96]{2,1,0:T(4,128)S(1)}, f32[1,4,96]{2,1,0:T(4,128)}, u32[]{:S(2)}) copy-start(f32[1,4,96]{2,1,0:T(4,128)} %param.21) | copy-start | bytes 4612
  21.1 42.2 %all-reduce.4.cloned.1.call-start = ((), (), s32[]{:S(2)}) async-start(), calls=%async_computation.3 | async-start | bytes 458752 | tf_op jit(solution)/shard_map/psum | solution.py:52
  21.8 66.3 %all-gather.7.cloned.1.call-start = ((), (), s32[]{:S(2)}) async-start(), calls=%async_computation.1 | async-start | bytes 5308416 | tf_op jit(solution)/shard_map/all_gather | solution.py:66
  51.8 77.6 %all-gather.5.cloned.1.call-start = ((), (), s32[]{:S(2)}) async-start(), calls=%async_computation | async-start | bytes 5308416 | tf_op jit(solution)/shard_map/all_gather | solution.py:65
  63.3 4.0 %copy-start.11 = (f32[384,64]{0,1:T(8,128)S(1)}, f32[384,64]{0,1:T(8,128)}, u32[]{:S(2)}) copy-start(f32[384,64]{0,1:T(8,128)} %get-tuple-element.14) | copy-start | bytes 294916
  67.3 103.4 %all-gather.9.cloned.1.call-start = ((), (), s32[]{:S(2)}) async-start(), calls=%async_computation.2 | async-start | bytes 5308416 | tf_op jit(solution)/shard_map/all_gather | solution.py:67
  67.3 3.9 %copy-start.14 = (f32[4,96]{1,0:T(4,128)S(1)}, f32[4,96]{1,0:T(4,128)}, u32[]{:S(2)}) copy-start(f32[4,96]{1,0:T(4,128)} %param.32) | copy-start | bytes 4612
  67.3 14.0 %copy-start.3 = (f32[96,3072]{1,0:T(8,128)S(1)}, f32[96,3072]{1,0:T(8,128)}, u32[]{:S(2)}) copy-start(f32[96,3072]{1,0:T(8,128)} %param.23) | copy-start | bytes 3538948
  170.7 5.2 %copy-start.4 = (bf16[768,3072]{1,0:T(8,128)(2,1)S(1)}, bf16[768,3072]{1,0:T(8,128)(2,1)}, u32[]{:S(2)}) copy-start(bf16[768,3072]{1,0:T(8,128)(2,1)} %all-gather.7.cloned.1.call-done) | copy-start | bytes 14155780
  170.7 8.0 %slice-start = ((s8[4718592]{0:T(1024)(128)(4,1)}), s8[4194304]{0:T(1024)(128)(4,1)S(1)}, s32[]{:S(2)}) async-start(s8[4718592]{0:T(1024)(128)(4,1)} %bitcast.63), calls=%async_computation.4 | async-start | bytes 8388608
  175.9 3.4 %slice-start.1 = ((s8[4718592]{0:T(1024)(128)(4,1)}), s8[524288]{0:T(1024)(128)(4,1)S(1)}, s32[]{:S(2)}) async-start(s8[4718592]{0:T(1024)(128)(4,1)} %bitcast.63), calls=%async_computation.5 | async-start | bytes 1048576
Sparse Core Ops, SparseCore 0:
  24.9 38.3 all-reduce.3
Sparse Core Ops, SparseCore 1:
  51.9 36.2 all-gather.6
  90.7 38.7 all-gather.4
  131.9 38.7 all-gather.8
where the time goes:
time: 189 us
  waiting for transfers between devices  97.4 us (52%)
  matrix products  31.5 us (17%)
  blocking collectives  30.9 us (16%)
  between operations  15.9 us (8%)
  local copies, waits for them, and re-layouts  12.6 us (7%)
    all_gather x1, waiting for transfers between devices, on_device(): lax.all_gather(owned_sq, 'shard', axis=1, tiled=True)  41.3 us
    all_gather x1, waiting for transfers between devices, on_device(): lax.all_gather(owned_down, 'shard', axis=0, tiled=True)  41.3 us
    psum x1, blocking collectives, on_device(): summed = lax.psum((factor_sq, factor_up, factor_down, norm_delta), 'rep')  22.1 us
    unnamed x38, local copies, waits for them, and re-layouts  12.6 us
    psum x1, waiting for transfers between devices, on_device(): summed = lax.psum((factor_sq, factor_up, factor_down, norm_delta), 'rep')  11.5 us
    all_gather x1, blocking collectives, on_device(): lax.all_gather(norm_weights, 'shard', axis=1, tiled=True)  8.85 us
    dot_general x1, matrix products, on_device(): outer_up = jnp.einsum('rk,fk->rf', mean_up, basis_up, precision=highest)  4.42 us
    dot_general x1, matrix products, on_device(): jnp.einsum('rk,fk->rf', factor_up, basis_up, precision=highest)  4.12 us
  transfers between devices with their start and end apart: 4, of which 4 were waited for; matrix products, arithmetic and copies ran while one was open for 11% of the time, Pallas kernels for 0%

commit v1 on v0

v1 whole, which is shorter than its diff:
```python
import functools

import jax
import jax.numpy as jnp
from jax import lax
from jax.experimental import pallas as pl
from jax.experimental.pallas import tpu as pltpu
from jax.sharding import PartitionSpec as P

moment_coef = 0.9
outer_rate = 0.7
MESH = pl.DeviceIdType.MESH
ANY = pl.BlockSpec(memory_space=pl.ANY)
VMEM = pl.BlockSpec(memory_space=pltpu.VMEM)
LANES = 128


def advance(start, moment, outer):
    new_moment = moment_coef * moment + outer
    weights = (start - outer_rate * (outer + moment_coef * new_moment)).astype(jnp.bfloat16)
    return (new_moment, weights)


def mean_kernel(groups, part_ref, mean_ref, landed, out_sem, in_sem, share_sem, got_sem):
    me, column = lax.axis_index("rep"), lax.axis_index("shard")
    barrier = pltpu.get_barrier_semaphore()
    peers = [lax.rem(me + step, groups) for step in range(1, groups)]
    for peer in peers:
        pl.semaphore_signal(barrier, inc=1, device_id=(peer, column), device_id_type=MESH)
    pl.semaphore_wait(barrier, groups - 1)
    scatter = [
        pltpu.make_async_remote_copy(
            part_ref.at[peer], landed.at[i], out_sem.at[i], in_sem.at[i],
            device_id=(peer, column), device_id_type=MESH,
        )
        for i, peer in enumerate(peers)
    ]
    for copy in scatter:
        copy.start()
    total = part_ref[me]
    for i, copy in enumerate(scatter):
        copy.wait_recv()
        total = total + landed[i]
    mean_ref[me] = total / groups
    share = [
        pltpu.make_async_remote_copy(
            mean_ref.at[me], mean_ref.at[me], share_sem.at[i], got_sem.at[i],
            device_id=(peer, column), device_id_type=MESH,
        )
        for i, peer in enumerate(peers)
    ]
    for copy in share:
        copy.start()
    for copy in scatter:
        copy.wait_send()
    for copy in share:
        copy.wait()


def mean_over_groups(part, groups):
    return pl.pallas_call(
        functools.partial(mean_kernel, groups),
        out_shape=jax.ShapeDtypeStruct(part.shape, part.dtype),
        in_specs=[VMEM],
        out_specs=VMEM,
        scratch_shapes=[pltpu.VMEM((groups - 1,) + part.shape[1:], part.dtype)]
        + [pltpu.SemaphoreType.DMA((groups - 1,))] * 4,
        compiler_params=pltpu.CompilerParams(collective_id=0, has_side_effects=True),
        name="mean_over_groups",
    )(part)


CHUNKS = 6


def gather_kernel(
    o_sq, o_up, o_dn, o_ln, w_sq, w_up, w_dn, w_ln,
    x_in, y_in, z_in, link_out, core_in, core_out, own_sem, ln_in, ln_out,
):
    plane, me = lax.axis_index("rep"), lax.axis_index("shard")
    parity = lax.rem(plane, 2)
    twin = plane + 1 - 2 * parity
    flip = lambda s, bit: s + bit - 2 * bit * lax.rem(s // bit, 2)
    side, across, sibling = flip(me, 2), flip(me, 4), flip(me, 1)
    corner = flip(side, 4)
    a, b = parity, 1 - parity

    barrier = pltpu.get_barrier_semaphore()
    mates = [lax.rem(me + step, 8) for step in range(1, 8)]
    for mate in mates:
        pl.semaphore_signal(barrier, inc=1, device_id=(plane, mate), device_id_type=MESH)
    pl.semaphore_signal(barrier, inc=1, device_id=(twin, me), device_id_type=MESH)
    pl.semaphore_wait(barrier, 8)

    rows = o_sq.shape[1]
    half = rows // 2
    width = o_sq.shape[2]
    deep = o_dn.shape[0]

    def piece(refs, owner, group, part, k):
        sq, up, dn = refs
        if k < 2:
            return sq.at[2 * group + k, pl.ds(pl.multiple_of(owner * rows + part * half, 16), half), :]
        if k < 4:
            return up.at[
                pl.ds(pl.multiple_of(owner * rows + part * half, 16), half),
                pl.ds(pl.multiple_of((2 * group + k - 2) * width, 128), width),
            ]
        return dn.at[
            pl.ds(pl.multiple_of(owner * deep + (4 * group + 2 * part + k - 4) * half, 16), half), :
        ]

    own, out = (o_sq, o_up, o_dn), (w_sq, w_up, w_dn)
    X, Y, Z = 0, 1, 2
    target = {X: (plane, side), Y: (plane, across), Z: (twin, me)}
    arrivals = {X: x_in, Y: y_in, Z: z_in}

    def send(way, kind, owner, group, part, k, mine=False):
        pltpu.make_async_remote_copy(
            piece(own, 0, group, part, k) if mine else piece(out, owner, group, part, k),
            piece(out, owner, group, part, k),
            link_out.at[way * 3 + k // 2],
            arrivals[way].at[kind * CHUNKS + k],
            device_id=target[way], device_id_type=MESH,
        ).start()

    def arrive(way, kind, owner, group, part, k):
        there = piece(out, owner, group, part, k)
        pltpu.make_async_copy(there, there, arrivals[way].at[kind * CHUNKS + k]).wait()
        pltpu.make_async_remote_copy(
            there, there, core_out.at[k // 2], core_in.at[k // 2],
            device_id=(plane, sibling), device_id_type=MESH,
        ).start()

    def first(k):
        send(X, 0, me, b, 0, k, True)
        send(Y, 0, me, b, 1, k, True)
        send(X, 1, me, a, 1, k, True)
        send(Y, 1, me, a, 0, k, True)

    def second(k):
        send(X, 3, me, a, 0, k, True)
        send(Y, 3, me, a, 1, k, True)

    first(0)
    second(0)
    first(1)

    homes = (
        w_sq.at[:, pl.ds(pl.multiple_of(me * rows, 16), rows), :],
        w_up.at[pl.ds(pl.multiple_of(me * rows, 16), rows), :],
        w_dn.at[pl.ds(pl.multiple_of(me * deep, 16), deep), :],
    )
    kept = [pltpu.make_async_copy(own[i], homes[i], own_sem.at[i]) for i in range(3)]
    kept.append(pltpu.make_async_copy(o_ln, w_ln.at[me], own_sem.at[3]))
    for copy in kept:
        copy.start()
    for i in range(3):
        pltpu.make_async_remote_copy(
            own[i], homes[i], core_out.at[i], core_in.at[i],
            device_id=(plane, sibling), device_id_type=MESH,
        ).start()
    norms = [
        pltpu.make_async_remote_copy(
            o_ln, w_ln.at[me], ln_out.at[i], ln_in.at[i],
            device_id=(plane, mate), device_id_type=MESH,
        )
        for i, mate in enumerate(mates)
    ]
    for copy in norms:
        copy.start()

    for k in range(CHUNKS + 2):
        if k < CHUNKS:
            arrive(X, 0, side, b, 0, k)
            send(Y, 2, side, b, 0, k)
            arrive(Y, 0, across, b, 1, k)
            send(X, 2, across, b, 1, k)
            arrive(X, 1, side, a, 1, k)
            send(Z, 2, side, a, 1, k)
            arrive(Y, 1, across, a, 0, k)
            send(Z, 3, across, a, 0, k)
            if k + 1 < CHUNKS:
                second(k + 1)
            if k + 2 < CHUNKS:
                first(k + 2)
        if 1 <= k <= CHUNKS:
            j = k - 1
            arrive(Y, 2, corner, b, 0, j)
            send(Z, 0, corner, b, 0, j)
            arrive(X, 2, corner, b, 1, j)
            send(Z, 1, corner, b, 1, j)
            arrive(X, 3, side, a, 0, j)
            arrive(Y, 3, across, a, 1, j)
        if k >= 2:
            j = k - 2
            arrive(Z, 2, side, b, 1, j)
            arrive(Z, 3, across, b, 0, j)
            arrive(Z, 0, corner, a, 0, j)
            arrive(Z, 1, corner, a, 1, j)

    for i in range(3):
        for way in range(3):
            pltpu.make_async_copy(own[i], own[i], link_out.at[way * 3 + i]).wait()
        share = (w_sq.at[:, pl.ds(0, 4 * rows), :], w_up.at[pl.ds(0, 4 * rows), :], w_dn.at[pl.ds(0, 4 * deep), :])[i]
        pltpu.make_async_copy(share, share, core_out.at[i]).wait()
        pltpu.make_async_copy(share, share, core_in.at[i]).wait()
    for copy in kept:
        copy.wait()
    for copy in norms:
        copy.wait()


def gather_weights(owned_sq, owned_up, owned_down, norm_weights, n):
    m, r, d = owned_sq.shape
    bf16 = jnp.bfloat16
    ln = jnp.pad(norm_weights, ((0, 16 - norm_weights.shape[0]), (0, LANES - norm_weights.shape[1])))
    dma = pltpu.SemaphoreType.DMA
    sq, up, down, lns = pl.pallas_call(
        gather_kernel,
        out_shape=[
            jax.ShapeDtypeStruct((m, n * r, d), bf16),
            jax.ShapeDtypeStruct((n * owned_up.shape[0], owned_up.shape[1]), bf16),
            jax.ShapeDtypeStruct((n * owned_down.shape[0], owned_down.shape[1]), bf16),
            jax.ShapeDtypeStruct((n,) + ln.shape, bf16),
        ],
        in_specs=[ANY] * 4,
        out_specs=[ANY] * 4,
        scratch_shapes=[
            dma((4 * CHUNKS,)), dma((4 * CHUNKS,)), dma((4 * CHUNKS,)),
            dma((9,)), dma((3,)), dma((3,)), dma((4,)), dma((7,)), dma((7,)),
        ],
        compiler_params=pltpu.CompilerParams(collective_id=1, has_side_effects=True),
        name="gather_weights",
    )(owned_sq, owned_up, owned_down, ln)
    lns = lns[:, : norm_weights.shape[0], : norm_weights.shape[1]]
    return sq, up, down, lns.transpose(1, 0, 2).reshape(norm_weights.shape[0], -1)


def on_device(
    trained_sq,
    trained_up,
    trained_down,
    trained_ln,
    start_sq,
    start_up,
    start_down,
    start_ln,
    resid_sq,
    resid_up,
    resid_down,
    mom_sq,
    mom_up,
    mom_down,
    mom_ln,
    basis_sq,
    basis_up,
    basis_down,
):
    fine = lax.Precision.HIGH
    groups = lax.axis_size("rep")
    shards = lax.axis_size("shard")
    delta_sq = start_sq - trained_sq[0] + resid_sq[0]
    factor_sq = jnp.einsum("mrd,mdk->mrk", delta_sq, basis_sq, precision=fine)
    delta_up = start_up - trained_up[0] + resid_up[0]
    factor_up = jnp.dot(delta_up, basis_up, precision=fine, preferred_element_type=jnp.float32)
    delta_down = start_down - trained_down[0] + resid_down[0]
    factor_down = jnp.dot(delta_down, basis_down, precision=fine, preferred_element_type=jnp.float32)
    norm_delta = start_ln - trained_ln[0]

    parts = (factor_sq, factor_up, factor_down, norm_delta)
    flat = jnp.concatenate([part.reshape(-1) for part in parts])
    slot = -(-flat.size // (groups * 8 * LANES)) * 8
    flat = jnp.pad(flat, (0, groups * slot * LANES - flat.size))
    mean = mean_over_groups(flat.reshape(groups, slot, LANES), groups).reshape(-1)
    means, at = [], 0
    for part in parts:
        means.append(mean[at : at + part.size].reshape(part.shape))
        at += part.size
    mean_sq, mean_up, mean_down, mean_ln = means

    new_resid_sq = delta_sq - jnp.einsum("mrk,mdk->mrd", factor_sq, basis_sq, precision=fine)
    new_resid_up = delta_up - jnp.einsum("rk,fk->rf", factor_up, basis_up, precision=fine)
    new_resid_down = delta_down - jnp.einsum("rk,dk->rd", factor_down, basis_down, precision=fine)
    new_mom_ln, norm_weights = advance(start_ln, mom_ln, mean_ln)
    outer_sq = jnp.einsum("mrk,mdk->mrd", mean_sq, basis_sq, precision=fine)
    outer_up = jnp.einsum("rk,fk->rf", mean_up, basis_up, precision=fine)
    outer_down = jnp.einsum("rk,dk->rd", mean_down, basis_down, precision=fine)
    new_mom_sq, owned_sq = advance(start_sq, mom_sq, outer_sq)
    new_mom_up, owned_up = advance(start_up, mom_up, outer_up)
    new_mom_down, owned_down = advance(start_down, mom_down, outer_down)
    if shards == 8 and groups % 2 == 0:
        weights = gather_weights(owned_sq, owned_up, owned_down, norm_weights, shards)
    else:
        weights = (
            lax.all_gather(owned_sq, "shard", axis=1, tiled=True),
            lax.all_gather(owned_up, "shard", axis=0, tiled=True),
            lax.all_gather(owned_down, "shard", axis=0, tiled=True),
            lax.all_gather(norm_weights, "shard", axis=1, tiled=True),
        )
    return (
        new_resid_sq[None],
        new_resid_up[None],
        new_resid_down[None],
        new_mom_sq,
        new_mom_up,
        new_mom_down,
        new_mom_ln,
        *weights,
    )


def solution(mesh):
    placed = (
        P("rep", None, "shard", None),
        P("rep", "shard", None),
        P("rep", "shard", None),
        P("rep", None, "shard"),
        P(None, "shard", None),
        P("shard", None),
        P("shard", None),
        P(None, "shard"),
        P("rep", None, "shard", None),
        P("rep", "shard", None),
        P("rep", "shard", None),
        P(None, "shard", None),
        P("shard", None),
        P("shard", None),
        P(None, "shard"),
        P(),
        P(),
        P(),
    )
    return jax.shard_map(
        on_device,
        mesh=mesh,
        in_specs=placed,
        out_specs=(
            P("rep", None, "shard", None),
            P("rep", "shard", None),
            P("rep", "shard", None),
            P(None, "shard", None),
            P("shard", None),
            P("shard", None),
            P(None, "shard"),
            P(),
            P(),
            P(),
            P(),
        ),
        check_vma=False,
    )
```

time: 189 us -> 129 us (0.68)
  waiting for transfers between devices: 97.4 us -> 0 us
  Pallas kernels: 0 us -> 75.5 us
  blocking collectives: 30.9 us -> 0 us
  between operations: 15.9 us -> 0.78 us
  local copies, waits for them, and re-layouts: 12.6 us -> 22.1 us
  matrix products: 31.5 us -> 26.9 us
  other arithmetic: 0.59 us -> 2.95 us
    all_gather x3 -> x0, waiting for transfers between devices: 85.2 us -> none  [the longest x1 41.3 us: on_device(): lax.all_gather(owned_sq, 'shard', axis=1, tiled=True)]
    pallas_call x0 -> x2, Pallas kernels: none -> 75.5 us  [the longest x1 58.2 us: gather_weights(): pl.pallas_call(gather_kernel, out_shape=[jax.ShapeDtypeStruct((m, n * r,...]
    psum x1 -> x0, blocking collectives: 22.1 us -> none  [on_device(): summed = lax.psum((factor_sq, factor_up, factor_down, norm_delta), 'rep')]
    psum x1 -> x0, waiting for transfers between devices: 11.5 us -> none  [on_device(): summed = lax.psum((factor_sq, factor_up, factor_down, norm_delta), 'rep')]
    all_gather x1 -> x0, blocking collectives: 8.85 us -> none  [on_device(): lax.all_gather(norm_weights, 'shard', axis=1, tiled=True)]
    reshape x0 -> x7, local copies, waits for them, and re-layouts: none -> 5.6 us  [the longest x4 3.17 us: on_device(): flat = jnp.concatenate([part.reshape(-1) for part in parts])]
    dot_general x9, matrix products: 31.5 us -> 26.9 us  [the longest x1 3.57 us: on_device(): jnp.einsum('mrk,mdk->mrd', factor_sq, basis_sq, precision=fine)]
    slice x0 -> x3, local copies, waits for them, and re-layouts: none -> 4.07 us  [on_device(): means.append(mean[at:at + part.size].reshape(part.shape))]
  transfers between devices with their start and end apart: 4 -> 0, of which waited for: 4 -> 0; matrix products, arithmetic and copies ran while one was open for 11% -> 0% of each run, Pallas kernels for 0% -> 0%
where the time goes in v1:
time: 129 us; the launch traced here: 128 us
  Pallas kernels  75.5 us (59%)
  matrix products  26.9 us (21%)
  local copies, waits for them, and re-layouts  22.1 us (17%)
  other arithmetic  2.95 us (2%)
    pallas_call x1, Pallas kernels, gather_weights(): pl.pallas_call(gather_kernel, out_shape=[jax.ShapeDtypeStruct((m, n * r,...  58.2 us
    pallas_call x1, Pallas kernels, mean_over_groups(): pl.pallas_call(functools.partial(mean_kernel, groups), out_shape=jax.Shap...  17.3 us
    unnamed x43, local copies, waits for them, and re-layouts  9.24 us
    slice x3, local copies, waits for them, and re-layouts, on_device(): means.append(mean[at:at + part.size].reshape(part.shape))  4.07 us
    dot_general x1, matrix products, on_device(): jnp.einsum('mrk,mdk->mrd', factor_sq, basis_sq, precision=fine)  3.57 us
    dot_general x1, matrix products, on_device(): jnp.einsum('rk,dk->rd', factor_down, basis_down, precision=fine)  3.56 us
    dot_general x1, matrix products, on_device(): outer_sq = jnp.einsum('mrk,mdk->mrd', mean_sq, basis_sq, precision=fine)  3.43 us
    reshape x4, local copies, waits for them, and re-layouts, on_device(): flat = jnp.concatenate([part.reshape(-1) for part in parts])  3.17 us

profile of v1, /device:TPU:0, one launch (start us, length us, event | category | flops | bytes accessed | tf_op | source)
XLA Modules:
  0.0 128.3 jit_solution(7923686031479882098)
XLA Ops:
  0.7 1.1 copy-done
  1.8 2.8 %fusion.7 = f32[4,96,64]{1,2,0:T(8,128)S(1)} fusion(f32[4,768,64]{1,2,0:T(8,128)S(1)} %copy-done, f32[1,4,96,768]{3,2,1,0:T(8,128)} %param.26, f32[4,96,768]{2,1,0:T(8,128)} %param.22, f32[1,4,96,768]{3,2,1,0:T(8,128)} %param.18), kind=kOutput, calls=%fused_computation.30 | convolution fusion | flops 113836032 | bytes 4423680 | tf_op jit(solution)/shard_map/mrd,mdk->mrk/dot_general | solution.py:264
  4.6 0.1 copy.29
  4.7 0.7 reshape.55
  5.4 3.0 %fusion.9 = f32[384,64]{0,1:T(8,128)} fusion(f32[768,64]{0,1:T(8,128)S(1)} %copy-done.11, f32[1,384,768]{2,1,0:T(8,128)} %param.28, f32[384,768]{1,0:T(8,128)S(1)} %copy-done.2, f32[1,384,768]{2,1,0:T(8,128)} %param.20), kind=kOutput, calls=%fused_computation.32 | convolution fusion | flops 113836032 | bytes 3833856 | tf_op jit(solution)/shard_map/dot_general | solution.py:268
  8.5 1.7 %copy.31 = f32[384,64]{1,0:T(8,128)} copy(f32[384,64]{0,1:T(8,128)} %fusion.9) | data formatting | bytes 196608 | tf_op jit(solution)/shard_map/dot_general | solution.py:268
  10.2 1.7 %reshape.57 = f32[24576]{0:T(1024)} reshape(f32[384,64]{1,0:T(8,128)} %copy.31) | data formatting | bytes 196608 | tf_op jit(solution)/shard_map/reshape | solution.py:272
  11.9 2.6 %fusion.8 = f32[96,64]{0,1:T(8,128)S(1)} fusion(f32[3072,64]{0,1:T(8,128)} %param.34, f32[1,96,3072]{2,1,0:T(8,128)} %param.27, f32[96,3072]{1,0:T(8,128)S(1)} %copy-done.3, f32[1,96,3072]{2,1,0:T(8,128)} %param.19), kind=kOutput, calls=%fused_computation.31 | convolution fusion | flops 113836032 | bytes 4349952 | tf_op jit(solution)/shard_map/dot_general | solution.py:266
  14.5 0.7 reshape.56
  15.2 0.7 bitcast_subtract_fusion.3
  16.0 1.7 %select_maximum_fusion = f32[57344]{0:T(1024)} fusion(f32[384]{0:T(512)S(1)} %reshape.58, f32[24576]{0:T(1024)} %reshape.57, f32[6144]{0:T(1024)} %reshape.56, f32[24576]{0:T(1024)} %reshape.55), kind=kLoop, calls=%fused_computation.18 | loop fusion | flops 458752 | bytes 452096 | tf_op jit(solution)/shard_map/concatenate | solution.py:272
  17.7 17.3 %mean_over_groups.1 = f32[4,112,128]{2,1,0:T(8,128)} custom-call(f32[4,112,128]{2,1,0:T(8,128)} %bitcast.67), custom_call_target="tpu_custom_call" | custom-call | tf_op jit(solution)/shard_map/mean_over_groups/pallas_call | solution.py:61
  35.0 1.8 %slice.20 = f32[896,64]{1,0:T(8,128)} reshape(f32[4,112,128]{2,1,0:T(8,128)} %mean_over_groups.1) | data formatting | bytes 458752 | tf_op jit(solution)/shard_map/slice | solution.py:278
  36.8 3.1 %subtract_convert_fusion = (bf16[384,768]{1,0:T(8,128)(2,1)}, f32[384,768]{1,0:T(8,128)}) fusion(f32[384,768]{1,0:T(8,128)S(1)} %copy-done.2, f32[384,768]{1,0:T(8,128)S(1)} %copy-done.13, f32[768,64]{0,1:T(8,128)S(1)} %copy-done.11, f32[896,64]{1,0:T(8,128)} %slice.20), kind=kOutput, calls=%fused_computation.12 | convolution fusion | flops 115310592 | bytes 4521984 | tf_op jit(solution)/shard_map/rk,dk->rd/dot_general | solution.py:288
  39.9 2.9 %subtract_convert_fusion.1 = (bf16[96,3072]{1,0:T(8,128)(2,1)}, f32[96,3072]{1,0:T(8,128)}) fusion(f32[96,3072]{1,0:T(8,128)S(1)} %copy-done.4, f32[96,3072]{1,0:T(8,128)S(1)} %copy-done.12, f32[3072,64]{0,1:T(8,128)S(1)} %copy-done.6, f32[896,64]{1,0:T(8,128)} %slice.20), kind=kOutput, calls=%fused_computation.13 | convolution fusion | flops 115310592 | bytes 4964352 | tf_op jit(solution)/shard_map/rk,fk->rf/dot_general | solution.py:287
  42.8 1.5 %slice.25 = f32[24576]{0:T(1024)} slice(f32[57344]{0:T(1024)} %bitcast.65), slice={[0:24576]} | slice | bytes 196608 | tf_op jit(solution)/shard_map/slice | solution.py:278
  44.4 1.7 %reshape.61 = f32[4,96,64]{2,1,0:T(8,128)} reshape(f32[24576]{0:T(1024)} %slice.25) | data formatting | bytes 196608 | tf_op jit(solution)/shard_map/reshape | solution.py:278
  46.1 3.4 %subtract_convert_fusion.2 = (bf16[4,96,768]{2,1,0:T(8,128)(2,1)}, f32[4,96,768]{2,1,0:T(8,128)}) fusion(f32[4,96,768]{2,1,0:T(8,128)S(1)} %copy-done.1, f32[4,96,768]{2,1,0:T(8,128)} %param.29, f32[4,96,64]{2,1,0:T(8,128)} %reshape.61, f32[4,768,64]{1,2,0:T(8,128)S(1)} %copy-done), kind=kOutput, calls=%fused_computation.14 | convolution fusion | flops 115310592 | bytes 5013504 | tf_op jit(solution)/shard_map/mrk,mdk->mrd/dot_general | solution.py:286
  49.5 0.7 slice.28
  50.3 0.6 subtract_convert_fusion.3
  50.8 0.6 pad.9.o_ln
  51.4 58.2 %gather_weights.1 = (bf16[4,768,768]{2,1,0:T(8,128)(2,1)}, bf16[768,3072]{1,0:T(8,128)(2,1)}, bf16[3072,768]{1,0:T(8,128)(2,1)}, bf16[8,16,128]{2,1,0:T(8,128)(2,1)}) custom-call(bf16[4,96,768]{2,1,0:T(8,128)(2,1)} %get-tuple-element.25.o_sq, bf16[96,3072]{1,0:T(8,128)(2,1)} %get-tuple-element.23.o_up, bf16[384,768]{1,0:T(8,128)(2,1)} %get-tuple-element.21.o_dn, ...), custom_call_target="tpu_custom_call" | custom-call | tf_op jit(solution)/shard_map/gather_weights/pallas_call | solution.py:219
  109.7 0.7 slice_bitcast_fusion
  110.4 0.7 reshape.63
  111.1 3.6 %fusion.2 = f32[1,4,96,768]{3,2,1,0:T(8,128)} fusion(f32[4,96,64]{1,2,0:T(8,128)S(1)} %fusion.7, f32[4,768,64]{1,2,0:T(8,128)S(1)} %copy-done, f32[1,4,96,768]{3,2,1,0:T(8,128)} %param.26, f32[4,96,768]{2,1,0:T(8,128)S(1)} %copy-done.1, f32[1,4,96,768]{3,2,1,0:T(8,128)} %param.18), kind=kOutput, calls=%fused_computation.5 | convolution fusion | flops 114130944 | bytes 5603328 | tf_op jit(solution)/shard_map/mrk,mdk->mrd/dot_general | solution.py:282
  114.7 3.6 %fusion.1 = f32[1,384,768]{2,1,0:T(8,128)} fusion(f32[384,64]{0,1:T(8,128)} %fusion.9, f32[768,64]{0,1:T(8,128)S(1)} %copy-done.11, f32[1,384,768]{2,1,0:T(8,128)} %param.28, f32[384,768]{1,0:T(8,128)S(1)} %copy-done.2, f32[1,384,768]{2,1,0:T(8,128)} %param.20), kind=kOutput, calls=%fused_computation.3 | convolution fusion | flops 114130944 | bytes 5013504 | tf_op jit(solution)/shard_map/rk,dk->rd/dot_general | solution.py:284
  118.3 2.0 %fusion = f32[1,96,3072]{2,1,0:T(8,128)} fusion(f32[96,64]{0,1:T(8,128)S(1)} %fusion.8, f32[3072,64]{0,1:T(8,128)S(1)} %copy-done.7, f32[1,96,3072]{2,1,0:T(8,128)S(1)} %copy-done.9, f32[96,3072]{1,0:T(8,128)S(1)} %copy-done.5, f32[1,96,3072]{2,1,0:T(8,128)S(1)} %copy-done.10), kind=kOutput, calls=%fused_computation.1 | convolution fusion | flops 114130944 | bytes 5529600 | tf_op jit(solution)/shard_map/rk,fk->rf/dot_general | solution.py:283
  120.2 2.4 %copy.38 = bf16[4,768,768]{2,1,0:T(8,128)(2,1)} copy(bf16[4,768,768]{2,1,0:T(8,128)(2,1)S(1)} %copy-done.8) | data formatting | bytes 9437184
  122.7 2.4 %copy.39 = bf16[768,3072]{1,0:T(8,128)(2,1)} copy(bf16[768,3072]{1,0:T(8,128)(2,1)S(1)} %bitcast.64) | data formatting | bytes 9437184
  125.1 0.4 slice-done
  125.5 0.7 slice-done.1
  126.1 2.2 %copy.40 = bf16[3072,768]{1,0:T(8,128)(2,1)} copy(bf16[3072,768]{1,0:T(8,128)(2,1)S(1)} %bitcast.62) | data formatting | bytes 9437184
  (43 shorter events, 0.3 us)
Async XLA Ops:
  0.6 1.1 copy-start
  0.7 4.8 %copy-start.11 = (f32[768,64]{0,1:T(8,128)S(1)}, f32[768,64]{0,1:T(8,128)}, u32[]{:S(2)}) copy-start(f32[768,64]{0,1:T(8,128)} %param.35) | copy-start | bytes 589828
  1.8 3.7 %copy-start.2 = (f32[384,768]{1,0:T(8,128)S(1)}, f32[384,768]{1,0:T(8,128)}, u32[]{:S(2)}) copy-start(f32[384,768]{1,0:T(8,128)} %param.24) | copy-start | bytes 3538948
  5.4 6.4 %copy-start.3 = (f32[96,3072]{1,0:T(8,128)S(1)}, f32[96,3072]{1,0:T(8,128)}, u32[]{:S(2)}) copy-start(f32[96,3072]{1,0:T(8,128)} %param.23) | copy-start | bytes 3538948
  14.4 22.4 %copy-start.13 = (f32[384,768]{1,0:T(8,128)S(1)}, f32[384,768]{1,0:T(8,128)}, u32[]{:S(2)}) copy-start(f32[384,768]{1,0:T(8,128)} %param.31) | copy-start | bytes 3538948
  36.8 3.1 %copy-start.4 = (f32[96,3072]{1,0:T(8,128)S(1)}, f32[96,3072]{1,0:T(8,128)}, u32[]{:S(2)}) copy-start(f32[96,3072]{1,0:T(8,128)} %param.23) | copy-start | bytes 3538948
  36.8 3.1 %copy-start.6 = (f32[3072,64]{0,1:T(8,128)S(1)}, f32[3072,64]{0,1:T(8,128)}, u32[]{:S(2)}) copy-start(f32[3072,64]{0,1:T(8,128)} %param.34) | copy-start | bytes 2359300
  36.8 3.1 %copy-start.12 = (f32[96,3072]{1,0:T(8,128)S(1)}, f32[96,3072]{1,0:T(8,128)}, u32[]{:S(2)}) copy-start(f32[96,3072]{1,0:T(8,128)} %param.30) | copy-start | bytes 3538948
  39.9 6.1 %copy-start.1 = (f32[4,96,768]{2,1,0:T(8,128)S(1)}, f32[4,96,768]{2,1,0:T(8,128)}, u32[]{:S(2)}) copy-start(f32[4,96,768]{2,1,0:T(8,128)} %param.22) | copy-start | bytes 3538948
  46.0 4.2 %copy-start.14 = (f32[4,96]{1,0:T(4,128)S(1)}, f32[4,96]{1,0:T(4,128)}, u32[]{:S(2)}) copy-start(f32[4,96]{1,0:T(4,128)} %param.25) | copy-start | bytes 4612
  46.1 4.2 %copy-start.15 = (f32[4,96]{1,0:T(4,128)S(1)}, f32[4,96]{1,0:T(4,128)}, u32[]{:S(2)}) copy-start(f32[4,96]{1,0:T(4,128)} %param.32) | copy-start | bytes 4612
  111.1 7.1 %copy-start.9 = (f32[1,96,3072]{2,1,0:T(8,128)S(1)}, f32[1,96,3072]{2,1,0:T(8,128)}, u32[]{:S(2)}) copy-start(f32[1,96,3072]{2,1,0:T(8,128)} %param.27) | copy-start | bytes 3538948
  111.1 7.1 %copy-start.10 = (f32[1,96,3072]{2,1,0:T(8,128)S(1)}, f32[1,96,3072]{2,1,0:T(8,128)}, u32[]{:S(2)}) copy-start(f32[1,96,3072]{2,1,0:T(8,128)} %param.19) | copy-start | bytes 3538948
  111.1 9.1 %copy-start.8 = (bf16[4,768,768]{2,1,0:T(8,128)(2,1)S(1)}, bf16[4,768,768]{2,1,0:T(8,128)(2,1)}, u32[]{:S(2)}) copy-start(bf16[4,768,768]{2,1,0:T(8,128)(2,1)} %get-tuple-element.45) | copy-start | bytes 14155780
  114.7 3.6 %copy-start.5 = (f32[96,3072]{1,0:T(8,128)S(1)}, f32[96,3072]{1,0:T(8,128)}, u32[]{:S(2)}) copy-start(f32[96,3072]{1,0:T(8,128)} %param.23) | copy-start | bytes 3538948
  114.7 3.6 %copy-start.7 = (f32[3072,64]{0,1:T(8,128)S(1)}, f32[3072,64]{0,1:T(8,128)}, u32[]{:S(2)}) copy-start(f32[3072,64]{0,1:T(8,128)} %param.34) | copy-start | bytes 2359300
  114.7 8.0 %slice-start.2 = ((s8[4718592]{0:T(1024)(128)(4,1)}), s8[4194304]{0:T(1024)(128)(4,1)S(1)}, s32[]{:S(2)}) async-start(s8[4718592]{0:T(1024)(128)(4,1)} %bitcast.63), calls=%async_computation.2 | async-start | bytes 8388608
  118.3 4.4 %slice-start.3 = ((s8[4718592]{0:T(1024)(128)(4,1)}), s8[524288]{0:T(1024)(128)(4,1)S(1)}, s32[]{:S(2)}) async-start(s8[4718592]{0:T(1024)(128)(4,1)} %bitcast.63), calls=%async_computation.3 | async-start | bytes 1048576
  120.2 5.2 %slice-start = ((s8[4718592]{0:T(1024)(128)(4,1)}), s8[4194304]{0:T(1024)(128)(4,1)S(1)}, s32[]{:S(2)}) async-start(s8[4718592]{0:T(1024)(128)(4,1)} %bitcast.61), calls=%async_computation | async-start | bytes 8388608
  122.6 3.5 %slice-start.1 = ((s8[4718592]{0:T(1024)(128)(4,1)}), s8[524288]{0:T(1024)(128)(4,1)S(1)}, s32[]{:S(2)}) async-start(s8[4718592]{0:T(1024)(128)(4,1)} %bitcast.61), calls=%async_computation.1 | async-start | bytes 1048576

commit v2 on v1

--- a/solution.py
+++ b/solution.py
@@ -73,10 +73,27 @@
 CHUNKS = 6
 
 
-def gather_kernel(
-    o_sq, o_up, o_dn, o_ln, w_sq, w_up, w_dn, w_ln,
+def halves(x):
+    top = x.astype(jnp.bfloat16)
+    return top, (x - top.astype(jnp.float32)).astype(jnp.bfloat16)
+
+
+def times(x, top, low, dims):
+    x_top, x_low = halves(x)
+    dot = lambda u, v: lax.dot_general(u, v, (dims, ((), ())), preferred_element_type=jnp.float32)
+    return dot(x_top, top) + (dot(x_top, low) + dot(x_low, top))
+
+
+def step_kernel(
+    t_sq, t_up, t_dn, s_sq, s_up, s_dn, r_sq, r_up, r_dn, m_sq, m_up, m_dn,
+    t_ln, s_ln, m_ln, basis_sq, basis_up, basis_dn,
+    nr_sq, nr_up, nr_dn, nm_sq, nm_up, nm_dn, nm_ln, w_sq, w_up, w_dn, w_ln,
+    vt_sq, vt_up, vt_dn, vs_sq, vs_up, vs_dn, vr_sq, vr_up, vr_dn, vm_sq, vm_up, vm_dn,
+    o_sq, o_up, o_dn, o_ln, wide, top, low, part, mean, landed,
+    load_sem, store_sem, out_sem, in_sem, share_sem, got_sem,
     x_in, y_in, z_in, link_out, core_in, core_out, own_sem, ln_in, ln_out,
 ):
+    groups = 4
     plane, me = lax.axis_index("rep"), lax.axis_index("shard")
     parity = lax.rem(plane, 2)
     twin = plane + 1 - 2 * parity
@@ -87,45 +104,168 @@
 
     barrier = pltpu.get_barrier_semaphore()
     mates = [lax.rem(me + step, 8) for step in range(1, 8)]
+    peers = [lax.rem(plane + step, groups) for step in range(1, groups)]
     for mate in mates:
         pl.semaphore_signal(barrier, inc=1, device_id=(plane, mate), device_id_type=MESH)
-    pl.semaphore_signal(barrier, inc=1, device_id=(twin, me), device_id_type=MESH)
-    pl.semaphore_wait(barrier, 8)
-
-    rows = o_sq.shape[1]
-    half = rows // 2
-    width = o_sq.shape[2]
-    deep = o_dn.shape[0]
-
-    def piece(refs, owner, group, part, k):
+    for peer in peers:
+        pl.semaphore_signal(barrier, inc=1, device_id=(peer, me), device_id_type=MESH)
+
+    loads = [
+        pltpu.make_async_copy(src, dst, load_sem.at[i])
+        for i, (src, dst) in enumerate([
+            (t_sq, vt_sq), (s_sq, vs_sq), (r_sq, vr_sq),
+            (t_dn, vt_dn), (s_dn, vs_dn), (r_dn, vr_dn),
+            (t_up, vt_up), (s_up, vs_up), (r_up, vr_up),
+            (m_sq, vm_sq), (m_up, vm_up), (m_dn, vm_dn),
+        ])
+    ]
+    for copy in loads:
+        copy.start()
+
+    rows, width = vs_sq.shape[1], vs_sq.shape[2]
+    half, deep, rank = rows // 2, vs_dn.shape[0], basis_dn.shape[1]
+    DN, UP = 4 * width, 6 * width
+    wide[...] = jnp.zeros_like(wide)
+
+    def lay(block, *places):
+        wide[:, :rank] = block
+        x = wide[...]
+        for place, high in places:
+            top[pl.ds(place, width), :], low[pl.ds(place, width), :] = halves(pltpu.roll(x, rank, 1) if high else x)
+
+    for m in range(4):
+        lay(basis_sq[m], (m * width, m % 2))
+    lay(basis_dn[...], (DN, 0), (DN + width, 1))
+    for c in range(4):
+        lay(basis_up[pl.ds(c * width, width), :], (UP + c * width, 0), (UP + (4 + c) * width, 1))
+
+    def factor(delta, place):
+        return times(delta, top[pl.ds(place, width), :], low[pl.ds(place, width), :], ((1,), (0,)))
+
+    for i in range(3):
+        loads[i].wait()
+    for pair in range(2):
+        total = None
+        for m in (2 * pair, 2 * pair + 1):
+            delta = vs_sq[m] - vt_sq[m] + vr_sq[m]
+            vr_sq[m] = delta
+            f = factor(delta, m * width)
+            total = f if total is None else total + f
+        part[pl.ds(pair * rows, rows), :] = total
+    for i in range(3, 6):
+        loads[i].wait()
+    for g in range(2):
+        total = None
+        for high in range(2):
+            at = pl.ds(high * (deep // 2) + g * rows, rows)
+            delta = vs_dn[at, :] - vt_dn[at, :] + vr_dn[at, :]
+            vr_dn[at, :] = delta
+            f = factor(delta, DN + high * width)
+            total = f if total is None else total + f
+        part[pl.ds(2 * rows + g * rows, rows), :] = total
+    for i in range(6, 9):
+        loads[i].wait()
+    total = None
+    for high in range(2):
+        for c in range(4):
+            at = (pl.ds(high * half, half), pl.ds(c * width, width))
+            delta = vs_up[at] - vt_up[at] + vr_up[at]
+            vr_up[at] = delta
+            f = factor(delta, UP + (4 * high + c) * width)
+            total = f if total is None else total + f
+    part[pl.ds(4 * rows, half), :] = total
+    tail = 4 * rows + half
+    part[pl.ds(tail, 16), :] = jnp.zeros((16, LANES), jnp.float32)
+    part[pl.ds(tail, 4), :rows] = s_ln[...] - t_ln[...]
+
+    pl.semaphore_wait(barrier, 10)
+    slot = part.shape[0] // groups
+    rows_of = lambda g: pl.ds(pl.multiple_of(g * slot, 8), slot)
+    scatter = [
+        pltpu.make_async_remote_copy(
+            part.at[rows_of(peer), :], landed.at[i], out_sem.at[i], in_sem.at[i],
+            device_id=(peer, me), device_id_type=MESH,
+        )
+        for i, peer in enumerate(peers)
+    ]
+    for copy in scatter:
+        copy.start()
+    total = part[rows_of(plane), :]
+    for i, copy in enumerate(scatter):
+        copy.wait_recv()
+        total = total + landed[i]
+    mean[rows_of(plane), :] = total / groups
+    share = [
+        pltpu.make_async_remote_copy(
+            mean.at[rows_of(plane), :], mean.at[rows_of(plane), :], share_sem.at[i], got_sem.at[i],
+            device_id=(peer, me), device_id_type=MESH,
+        )
+        for i, peer in enumerate(peers)
+    ]
+    for copy in share:
+        copy.start()
+    for i in range(9, 12):
+        loads[i].wait()
+    for copy in scatter:
+        copy.wait_send()
+    for copy in share:
+        copy.wait()
+
+    def piece(refs, owner, group, part_, k):
         sq, up, dn = refs
         if k < 2:
-            return sq.at[2 * group + k, pl.ds(pl.multiple_of(owner * rows + part * half, 16), half), :]
+            return sq.at[2 * group + k, pl.ds(pl.multiple_of(owner * rows + part_ * half, 16), half), :]
         if k < 4:
             return up.at[
-                pl.ds(pl.multiple_of(owner * rows + part * half, 16), half),
+                pl.ds(pl.multiple_of(owner * rows + part_ * half, 16), half),
                 pl.ds(pl.multiple_of((2 * group + k - 2) * width, 128), width),
             ]
         return dn.at[
-            pl.ds(pl.multiple_of(owner * deep + (4 * group + 2 * part + k - 4) * half, 16), half), :
+            pl.ds(pl.multiple_of(owner * deep + (4 * group + 2 * part_ + k - 4) * half, 16), half), :
         ]
 
+    def places(group, h, k):
+        if k < 2:
+            return group * rows + h * half, (2 * group + k) * width
+        if k < 4:
+            return 4 * rows, UP + (4 * h + 2 * group + k - 2) * width
+        return 2 * rows + (2 * h + k - 4) * half, DN + group * width
+
+    def spread(ref, group, h, k):
+        row, place = places(group, h, k)
+        row = row if isinstance(row, int) else pl.multiple_of(row, 16)
+        at = pl.ds(pl.multiple_of(place, 16), width)
+        return times(ref[pl.ds(row, half), :], top[at, :], low[at, :], ((1,), (1,)))
+
+    vs, vr, vm = (vs_sq, vs_up, vs_dn), (vr_sq, vr_up, vr_dn), (vm_sq, vm_up, vm_dn)
     own, out = (o_sq, o_up, o_dn), (w_sq, w_up, w_dn)
+
+    def update(group, h, k):
+        outer = spread(mean, group, h, k)
+        moment = piece(vm, 0, group, h, k)
+        new_moment, weights = advance(piece(vs, 0, group, h, k)[...], moment[...], outer)
+        moment[...] = new_moment
+        piece(own, 0, group, h, k)[...] = weights
+
+    def leave(group, h, k):
+        delta = piece(vr, 0, group, h, k)
+        delta[...] = delta[...] - spread(part, group, h, k)
+
     X, Y, Z = 0, 1, 2
     target = {X: (plane, side), Y: (plane, across), Z: (twin, me)}
     arrivals = {X: x_in, Y: y_in, Z: z_in}
 
-    def send(way, kind, owner, group, part, k, mine=False):
-        pltpu.make_async_remote_copy(
-            piece(own, 0, group, part, k) if mine else piece(out, owner, group, part, k),
-            piece(out, owner, group, part, k),
+    def send(way, kind, owner, group, h, k, mine=False):
+        pltpu.make_async_remote_copy(
+            piece(own, 0, group, h, k) if mine else piece(out, owner, group, h, k),
+            piece(out, owner, group, h, k),
             link_out.at[way * 3 + k // 2],
             arrivals[way].at[kind * CHUNKS + k],
             device_id=target[way], device_id_type=MESH,
         ).start()
 
-    def arrive(way, kind, owner, group, part, k):
-        there = piece(out, owner, group, part, k)
+    def arrive(way, kind, owner, group, h, k):
+        there = piece(out, owner, group, h, k)
         pltpu.make_async_copy(there, there, arrivals[way].at[kind * CHUNKS + k]).wait()
         pltpu.make_async_remote_copy(
             there, there, core_out.at[k // 2], core_in.at[k // 2],
@@ -133,18 +273,34 @@
         ).start()
 
     def first(k):
+        update(b, 0, k)
         send(X, 0, me, b, 0, k, True)
+        update(b, 1, k)
         send(Y, 0, me, b, 1, k, True)
+        update(a, 1, k)
         send(X, 1, me, a, 1, k, True)
+        update(a, 0, k)
         send(Y, 1, me, a, 0, k, True)
 
     def second(k):
         send(X, 3, me, a, 0, k, True)
         send(Y, 3, me, a, 1, k, True)
 
-    first(0)
-    second(0)
-    first(1)
+    for k in range(3):
+        first(k)
+    nm_value, ln_value = advance(s_ln[...], m_ln[...], mean[pl.ds(tail, 4), :][:, :rows])
+    nm_ln[...] = nm_value
+    o_ln[...] = jnp.zeros_like(o_ln)
+    o_ln[:4, :rows] = ln_value
+    norms = [
+        pltpu.make_async_remote_copy(
+            o_ln, w_ln.at[me], ln_out.at[i], ln_in.at[i],
+            device_id=(plane, mate), device_id_type=MESH,
+        )
+        for i, mate in enumerate(mates)
+    ]
+    for copy in norms:
+        copy.start()
 
     homes = (
         w_sq.at[:, pl.ds(pl.multiple_of(me * rows, 16), rows), :],
@@ -153,22 +309,12 @@
     )
     kept = [pltpu.make_async_copy(own[i], homes[i], own_sem.at[i]) for i in range(3)]
     kept.append(pltpu.make_async_copy(o_ln, w_ln.at[me], own_sem.at[3]))
-    for copy in kept:
-        copy.start()
-    for i in range(3):
-        pltpu.make_async_remote_copy(
-            own[i], homes[i], core_out.at[i], core_in.at[i],
-            device_id=(plane, sibling), device_id_type=MESH,
-        ).start()
-    norms = [
-        pltpu.make_async_remote_copy(
-            o_ln, w_ln.at[me], ln_out.at[i], ln_in.at[i],
-            device_id=(plane, mate), device_id_type=MESH,
-        )
-        for i, mate in enumerate(mates)
-    ]
-    for copy in norms:
-        copy.start()
+    stores = [
+        pltpu.make_async_copy(src, dst, store_sem.at[i])
+        for i, (src, dst) in enumerate([
+            (vm_sq, nm_sq), (vm_up, nm_up), (vm_dn, nm_dn), (vr_sq, nr_sq), (vr_up, nr_up), (vr_dn, nr_dn),
+        ])
+    ]
 
     for k in range(CHUNKS + 2):
         if k < CHUNKS:
@@ -180,61 +326,83 @@
             send(Z, 2, side, a, 1, k)
             arrive(Y, 1, across, a, 0, k)
             send(Z, 3, across, a, 0, k)
-            if k + 1 < CHUNKS:
-                second(k + 1)
-            if k + 2 < CHUNKS:
-                first(k + 2)
         if 1 <= k <= CHUNKS:
             j = k - 1
             arrive(Y, 2, corner, b, 0, j)
             send(Z, 0, corner, b, 0, j)
             arrive(X, 2, corner, b, 1, j)
             send(Z, 1, corner, b, 1, j)
-            arrive(X, 3, side, a, 0, j)
-            arrive(Y, 3, across, a, 1, j)
-        if k >= 2:
-            j = k - 2
-            arrive(Z, 2, side, b, 1, j)
-            arrive(Z, 3, across, b, 0, j)
-            arrive(Z, 0, corner, a, 0, j)
-            arrive(Z, 1, corner, a, 1, j)
+        if k + 3 < CHUNKS:
+            first(k + 3)
+        for j in {3: (0,), 4: (1, 2), 5: (3, 4, 5)}.get(k, ()):
+            second(j)
+        if k == 3:
+            for i in range(3):
+                kept[i].start()
+                stores[i].start()
+                pltpu.make_async_remote_copy(
+                    own[i], homes[i], core_out.at[i], core_in.at[i],
+                    device_id=(plane, sibling), device_id_type=MESH,
+                ).start()
+            kept[3].start()
+        if k < CHUNKS:
+            for group in range(2):
+                for h in range(2):
+                    leave(group, h, k)
+            if k % 2:
+                stores[3 + k // 2].start()
+
+    for j in range(CHUNKS):
+        arrive(Z, 2, side, b, 1, j)
+        arrive(Z, 3, across, b, 0, j)
+        arrive(Z, 0, corner, a, 0, j)
+        arrive(Z, 1, corner, a, 1, j)
+        arrive(X, 3, side, a, 0, j)
+        arrive(Y, 3, across, a, 1, j)
 
     for i in range(3):
         for way in range(3):
             pltpu.make_async_copy(own[i], own[i], link_out.at[way * 3 + i]).wait()
-        share = (w_sq.at[:, pl.ds(0, 4 * rows), :], w_up.at[pl.ds(0, 4 * rows), :], w_dn.at[pl.ds(0, 4 * deep), :])[i]
-        pltpu.make_async_copy(share, share, core_out.at[i]).wait()
-        pltpu.make_async_copy(share, share, core_in.at[i]).wait()
-    for copy in kept:
+        share_ = (w_sq.at[:, pl.ds(0, 4 * rows), :], w_up.at[pl.ds(0, 4 * rows), :], w_dn.at[pl.ds(0, 4 * deep), :])[i]
+        pltpu.make_async_copy(share_, share_, core_out.at[i]).wait()
+        pltpu.make_async_copy(share_, share_, core_in.at[i]).wait()
+    for copy in kept + norms + stores:
         copy.wait()
-    for copy in norms:
-        copy.wait()
-
-
-def gather_weights(owned_sq, owned_up, owned_down, norm_weights, n):
-    m, r, d = owned_sq.shape
-    bf16 = jnp.bfloat16
-    ln = jnp.pad(norm_weights, ((0, 16 - norm_weights.shape[0]), (0, LANES - norm_weights.shape[1])))
-    dma = pltpu.SemaphoreType.DMA
-    sq, up, down, lns = pl.pallas_call(
-        gather_kernel,
-        out_shape=[
-            jax.ShapeDtypeStruct((m, n * r, d), bf16),
-            jax.ShapeDtypeStruct((n * owned_up.shape[0], owned_up.shape[1]), bf16),
-            jax.ShapeDtypeStruct((n * owned_down.shape[0], owned_down.shape[1]), bf16),
-            jax.ShapeDtypeStruct((n,) + ln.shape, bf16),
+
+
+def whole_step(trained, start, resid, moment, norms, bases, n):
+    f32, bf16, dma = jnp.float32, jnp.bfloat16, pltpu.SemaphoreType.DMA
+    shape = jax.ShapeDtypeStruct
+    sq, up, dn = (x.shape for x in start)
+    tall = 14 * sq[2]
+    held = [pltpu.VMEM(x, f32) for x in (sq, up, dn)]
+    results = pl.pallas_call(
+        step_kernel,
+        out_shape=[shape(x, f32) for x in (sq, up, dn, sq, up, dn, norms[0].shape)]
+        + [
+            shape((sq[0], n * sq[1], sq[2]), bf16),
+            shape((n * up[0], up[1]), bf16),
+            shape((n * dn[0], dn[1]), bf16),
+            shape((n, 16, LANES), bf16),
         ],
-        in_specs=[ANY] * 4,
-        out_specs=[ANY] * 4,
-        scratch_shapes=[
-            dma((4 * CHUNKS,)), dma((4 * CHUNKS,)), dma((4 * CHUNKS,)),
-            dma((9,)), dma((3,)), dma((3,)), dma((4,)), dma((7,)), dma((7,)),
-        ],
-        compiler_params=pltpu.CompilerParams(collective_id=1, has_side_effects=True),
-        name="gather_weights",
-    )(owned_sq, owned_up, owned_down, ln)
-    lns = lns[:, : norm_weights.shape[0], : norm_weights.shape[1]]
-    return sq, up, down, lns.transpose(1, 0, 2).reshape(norm_weights.shape[0], -1)
+        in_specs=[ANY] * 12 + [VMEM] * 6,
+        out_specs=[ANY] * 6 + [VMEM] + [ANY] * 4,
+        scratch_shapes=held * 4
+        + [pltpu.VMEM(x, bf16) for x in (sq, up, dn, (16, LANES))]
+        + [pltpu.VMEM((sq[2], LANES), f32), pltpu.VMEM((tall, LANES), bf16), pltpu.VMEM((tall, LANES), bf16)]
+        + [pltpu.VMEM((448, LANES), f32), pltpu.VMEM((448, LANES), f32), pltpu.VMEM((3, 112, LANES), f32)]
+        + [dma((12,)), dma((6,)), dma((3,)), dma((3,)), dma((3,)), dma((3,))]
+        + [dma((4 * CHUNKS,))] * 3
+        + [dma((9,)), dma((3,)), dma((3,)), dma((4,)), dma((7,)), dma((7,))],
+        compiler_params=pltpu.CompilerParams(
+            collective_id=1, has_side_effects=True, vmem_limit_bytes=56 * 2**20
+        ),
+        name="whole_step",
+    )(*trained, *start, *resid, *moment, *norms, *bases)
+    *rest, lns = results
+    lns = lns[:, : norms[0].shape[0], : norms[0].shape[1]].transpose(1, 0, 2).reshape(norms[0].shape[0], -1)
+    nr = [x[None] for x in rest[:3]]
+    return (*nr, *rest[3:], lns)
 
 
 def on_device(
@@ -260,6 +428,16 @@
     fine = lax.Precision.HIGH
     groups = lax.axis_size("rep")
     shards = lax.axis_size("shard")
+    if shards == 8 and groups == 4 and basis_down.shape[1] * 2 == LANES:
+        return whole_step(
+            (trained_sq[0], trained_up[0], trained_down[0]),
+            (start_sq, start_up, start_down),
+            (resid_sq[0], resid_up[0], resid_down[0]),
+            (mom_sq, mom_up, mom_down),
+            (trained_ln[0], start_ln, mom_ln),
+            (basis_sq, basis_up, basis_down),
+            shards,
+        )
     delta_sq = start_sq - trained_sq[0] + resid_sq[0]
     factor_sq = jnp.einsum("mrd,mdk->mrk", delta_sq, basis_sq, precision=fine)
     delta_up = start_up - trained_up[0] + resid_up[0]
@@ -289,15 +467,12 @@
     new_mom_sq, owned_sq = advance(start_sq, mom_sq, outer_sq)
     new_mom_up, owned_up = advance(start_up, mom_up, outer_up)
     new_mom_down, owned_down = advance(start_down, mom_down, outer_down)
-    if shards == 8 and groups % 2 == 0:
-        weights = gather_weights(owned_sq, owned_up, owned_down, norm_weights, shards)
-    else:
-        weights = (
-            lax.all_gather(owned_sq, "shard", axis=1, tiled=True),
-            lax.all_gather(owned_up, "shard", axis=0, tiled=True),
-            lax.all_gather(owned_down, "shard", axis=0, tiled=True),
-            lax.all_gather(norm_weights, "shard", axis=1, tiled=True),
-        )
+    weights = (
+        lax.all_gather(owned_sq, "shard", axis=1, tiled=True),
+        lax.all_gather(owned_up, "shard", axis=0, tiled=True),
+        lax.all_gather(owned_down, "shard", axis=0, tiled=True),
+        lax.all_gather(norm_weights, "shard", axis=1, tiled=True),
+    )
     return (
         new_resid_sq[None],
         new_resid_up[None],

time: 129 us -> 96.9 us (0.75)
  matrix products: 26.9 us -> 0 us
  Pallas kernels: 75.5 us -> 69.9 us
  local copies, waits for them, and re-layouts: 22.1 us -> 26.1 us
  other arithmetic: 2.95 us -> 0.01 us
    dot_general x9 -> x0, matrix products: 26.9 us -> none  [the longest x1 3.57 us: on_device(): jnp.einsum('mrk,mdk->mrd', factor_sq, basis_sq, precision=fine)]
    unnamed x43 -> x35, local copies, waits for them, and re-layouts: 9.24 us -> 24.7 us
    pallas_call x2 -> x1, Pallas kernels: 75.5 us -> 69.9 us  [whole_step(): pl.pallas_call(step_kernel, out_shape=[shape(x, f32) for x in (sq, up, dn...]
    reshape x7 -> x1, local copies, waits for them, and re-layouts: 5.6 us -> 0.68 us  [whole_step(): lns[:, :norms[0].shape[0], :norms[0].shape[1]].transpose(1, 0, 2)]
    slice x3 -> x0, local copies, waits for them, and re-layouts: 4.07 us -> none  [on_device(): means.append(mean[at:at + part.size].reshape(part.shape))]
    dot_general x3 -> x0, local copies, waits for them, and re-layouts: 1.9 us -> none  [the longest x1 1.7 us: on_device(): jnp.dot(delta_down, basis_down, precision=fine, preferred_element_type=jn...]
    concatenate x1 -> x0, other arithmetic: 1.66 us -> none  [on_device(): flat = jnp.concatenate([part.reshape(-1) for part in parts])]
where the time goes in v2:
time: 96.9 us; the launch traced here: 96.7 us
  Pallas kernels  69.9 us (72%)
  local copies, waits for them, and re-layouts  26.1 us (27%)
    pallas_call x1, Pallas kernels, whole_step(): pl.pallas_call(step_kernel, out_shape=[shape(x, f32) for x in (sq, up, dn...  69.9 us
    unnamed x35, local copies, waits for them, and re-layouts  24.7 us

profile of v2, /device:TPU:0, one launch (start us, length us, event | category | flops | bytes accessed | tf_op | source)
XLA Modules:
  0.0 96.7 jit_solution(9559463209313138334)
XLA Ops:
  0.6 1.8 %copy.34.basis_dn = f32[768,64]{1,0:T(8,128)} copy(f32[768,64]{0,1:T(8,128)} %param.35) | data formatting | bytes 393216 | tf_op args[17]
  2.5 0.0 copy-start.5
  2.5 2.8 %copy.32.basis_sq = f32[4,768,64]{2,1,0:T(8,128)} copy(f32[4,768,64]{1,2,0:T(8,128)} %param.33) | data formatting | bytes 1572864 | tf_op args[15]
  5.3 0.0 copy-done.5
  5.3 1.6 %copy.33.basis_up = f32[3072,64]{1,0:T(8,128)} copy(f32[3072,64]{0,1:T(8,128)S(1)} %copy-done.5) | data formatting | bytes 1572864 | tf_op args[16]
  6.9 69.9 %whole_step.1 = (f32[4,96,768]{2,1,0:T(8,128)}, f32[96,3072]{1,0:T(8,128)}, f32[384,768]{1,0:T(8,128)}, f32[4,96,768]{2,1,0:T(8,128)}, f32[96,3072]{1,0:T(8,128)...) custom-call(f32[4,96,768]{2,1,0:T(8,128)} %bitcast.16, ...), custom_call_target="tpu_custom_call" | custom-call | tf_op jit(solution)/shard_map/whole_step/pallas_call | solution.py:379
  76.9 0.7 slice_bitcast_fusion
  77.6 0.7 reshape.25
  78.3 0.0 copy-start.4
  78.3 0.0 copy-start.3
  78.3 2.5 %copy.46 = f32[1,4,96,768]{3,2,1,0:T(8,128)} copy(f32[1,4,96,768]{3,2,1,0:T(8,128)} %bitcast.24) | data formatting | bytes 2359296
  80.8 0.0 copy-start.2
  80.8 0.0 copy-start.1
  80.8 2.5 %copy.47 = f32[1,96,3072]{2,1,0:T(8,128)} copy(f32[1,96,3072]{2,1,0:T(8,128)} %bitcast.23) | data formatting | bytes 2359296
  83.3 0.0 copy-done.4
  83.3 1.0 %copy.48 = f32[1,384,768]{2,1,0:T(8,128)} copy(f32[1,384,768]{2,1,0:T(8,128)S(1)} %bitcast.22) | data formatting | bytes 2359296
  84.3 0.0 copy-done.3
  84.3 1.0 %copy.49 = f32[4,96,768]{2,1,0:T(8,128)} copy(f32[4,96,768]{2,1,0:T(8,128)S(1)} %copy-done.3) | data formatting | bytes 2359296
  85.3 0.0 copy-done.2
  85.3 1.0 %copy.50 = f32[96,3072]{1,0:T(8,128)} copy(f32[96,3072]{1,0:T(8,128)S(1)} %copy-done.2) | data formatting | bytes 2359296
  86.4 0.0 copy-done.1
  86.4 1.0 %copy.51 = f32[384,768]{1,0:T(8,128)} copy(f32[384,768]{1,0:T(8,128)S(1)} %copy-done.1) | data formatting | bytes 2359296
  87.4 0.0 copy-done.6
  87.4 0.6 copy.52
  88.0 0.7 copy-done
  88.6 2.4 %copy.53 = bf16[4,768,768]{2,1,0:T(8,128)(2,1)} copy(bf16[4,768,768]{2,1,0:T(8,128)(2,1)S(1)} %copy-done) | data formatting | bytes 9437184
  91.0 0.0 slice-done.2
  91.0 0.0 slice-done.3
  91.0 2.4 %copy.54 = bf16[768,3072]{1,0:T(8,128)(2,1)} copy(bf16[768,3072]{1,0:T(8,128)(2,1)S(1)} %bitcast.15) | data formatting | bytes 9437184
  93.4 0.4 slice-done
  93.9 0.6 slice-done.1
  94.5 2.2 %copy.55 = bf16[3072,768]{1,0:T(8,128)(2,1)} copy(bf16[3072,768]{1,0:T(8,128)(2,1)S(1)} %bitcast.13) | data formatting | bytes 9437184
  (9 shorter events, 0.0 us)
Async XLA Ops:
  2.5 2.8 %copy-start.5 = (f32[3072,64]{0,1:T(8,128)S(1)}, f32[3072,64]{0,1:T(8,128)}, u32[]{:S(2)}) copy-start(f32[3072,64]{0,1:T(8,128)} %param.34) | copy-start | bytes 2359300
  78.3 5.0 %copy-start.4 = (f32[384,768]{1,0:T(8,128)S(1)}, f32[384,768]{1,0:T(8,128)}, u32[]{:S(2)}) copy-start(f32[384,768]{1,0:T(8,128)} %get-tuple-element.24) | copy-start | bytes 3538948
  78.3 6.0 %copy-start.3 = (f32[4,96,768]{2,1,0:T(8,128)S(1)}, f32[4,96,768]{2,1,0:T(8,128)}, u32[]{:S(2)}) copy-start(f32[4,96,768]{2,1,0:T(8,128)} %get-tuple-element.47) | copy-start | bytes 3538948
  80.8 4.6 %copy-start.2 = (f32[96,3072]{1,0:T(8,128)S(1)}, f32[96,3072]{1,0:T(8,128)}, u32[]{:S(2)}) copy-start(f32[96,3072]{1,0:T(8,128)} %get-tuple-element.48) | copy-start | bytes 3538948
  80.8 5.6 %copy-start.1 = (f32[384,768]{1,0:T(8,128)S(1)}, f32[384,768]{1,0:T(8,128)}, u32[]{:S(2)}) copy-start(f32[384,768]{1,0:T(8,128)} %get-tuple-element.49) | copy-start | bytes 3538948
  83.3 7.7 %slice-start.2 = ((s8[4718592]{0:T(1024)(128)(4,1)}), s8[4194304]{0:T(1024)(128)(4,1)S(1)}, s32[]{:S(2)}) async-start(s8[4718592]{0:T(1024)(128)(4,1)} %bitcast.14), calls=%async_computation.2 | async-start | bytes 8388608
  84.3 3.1 %copy-start.6 = (f32[4,96]{1,0:T(4,128)S(1)}, f32[4,96]{1,0:T(4,128)}, u32[]{:S(2)}) copy-start(f32[4,96]{1,0:T(4,128)} %get-tuple-element.50) | copy-start | bytes 4612
  85.3 3.3 %copy-start = (bf16[4,768,768]{2,1,0:T(8,128)(2,1)S(1)}, bf16[4,768,768]{2,1,0:T(8,128)(2,1)}, u32[]{:S(2)}) copy-start(bf16[4,768,768]{2,1,0:T(8,128)(2,1)} %get-tuple-element.51) | copy-start | bytes 14155780
  87.4 3.6 %slice-start.3 = ((s8[4718592]{0:T(1024)(128)(4,1)}), s8[524288]{0:T(1024)(128)(4,1)S(1)}, s32[]{:S(2)}) async-start(s8[4718592]{0:T(1024)(128)(4,1)} %bitcast.14), calls=%async_computation.3 | async-start | bytes 1048576
  88.6 5.3 %slice-start = ((s8[4718592]{0:T(1024)(128)(4,1)}), s8[4194304]{0:T(1024)(128)(4,1)S(1)}, s32[]{:S(2)}) async-start(s8[4718592]{0:T(1024)(128)(4,1)} %bitcast.12), calls=%async_computation | async-start | bytes 8388608
  91.0 3.5 %slice-start.1 = ((s8[4718592]{0:T(1024)(128)(4,1)}), s8[524288]{0:T(1024)(128)(4,1)S(1)}, s32[]{:S(2)}) async-start(s8[4718592]{0:T(1024)(128)(4,1)} %bitcast.12), calls=%async_computation.1 | async-start | bytes 1048576

commit v3 on v2

--- a/solution.py
+++ b/solution.py
@@ -123,7 +123,7 @@
         copy.start()
 
     rows, width = vs_sq.shape[1], vs_sq.shape[2]
-    half, deep, rank = rows // 2, vs_dn.shape[0], basis_dn.shape[1]
+    half, deep, rank = rows // 2, vs_dn.shape[0], basis_dn.shape[0]
     DN, UP = 4 * width, 6 * width
     wide[...] = jnp.zeros_like(wide)
 
@@ -134,10 +134,10 @@
             top[pl.ds(place, width), :], low[pl.ds(place, width), :] = halves(pltpu.roll(x, rank, 1) if high else x)
 
     for m in range(4):
-        lay(basis_sq[m], (m * width, m % 2))
-    lay(basis_dn[...], (DN, 0), (DN + width, 1))
+        lay(basis_sq[m].T, (m * width, m % 2))
+    lay(basis_dn[...].T, (DN, 0), (DN + width, 1))
     for c in range(4):
-        lay(basis_up[pl.ds(c * width, width), :], (UP + c * width, 0), (UP + (4 + c) * width, 1))
+        lay(basis_up[:, pl.ds(c * width, width)].T, (UP + c * width, 0), (UP + (4 + c) * width, 1))
 
     def factor(delta, place):
         return times(delta, top[pl.ds(place, width), :], low[pl.ds(place, width), :], ((1,), (0,)))
@@ -435,7 +435,7 @@
             (resid_sq[0], resid_up[0], resid_down[0]),
             (mom_sq, mom_up, mom_down),
             (trained_ln[0], start_ln, mom_ln),
-            (basis_sq, basis_up, basis_down),
+            tuple(jnp.swapaxes(x, -1, -2) for x in (basis_sq, basis_up, basis_down)),
             shards,
         )
     delta_sq = start_sq - trained_sq[0] + resid_sq[0]

time: 96.9 us -> 90.2 us (0.931)
  local copies, waits for them, and re-layouts: 26.1 us -> 19.8 us
    unnamed x35 -> x30, local copies, waits for them, and re-layouts: 24.7 us -> 18.4 us
where the time goes in v3:
time: 90.2 us; the launch traced here: 90 us
  Pallas kernels  69.5 us (77%)
  local copies, waits for them, and re-layouts  19.8 us (22%)
    pallas_call x1, Pallas kernels, whole_step(): pl.pallas_call(step_kernel, out_shape=[shape(x, f32) for x in (sq, up, dn...  69.5 us
    unnamed x30, local copies, waits for them, and re-layouts  18.4 us

profile of v3, /device:TPU:0, one launch (start us, length us, event | category | flops | bytes accessed | tf_op | source)
XLA Modules:
  0.0 90.0 jit_solution(5223318849594713757)
XLA Ops:
  0.7 69.5 %whole_step.1 = (f32[4,96,768]{2,1,0:T(8,128)}, f32[96,3072]{1,0:T(8,128)}, f32[384,768]{1,0:T(8,128)}, f32[4,96,768]{2,1,0:T(8,128)}, f32[96,3072]{1,0:T(8,128)...) custom-call(f32[4,96,768]{2,1,0:T(8,128)} %bitcast.19, ...), custom_call_target="tpu_custom_call" | custom-call | tf_op jit(solution)/shard_map/whole_step/pallas_call | solution.py:379
  70.1 0.7 slice_bitcast_fusion
  70.9 0.7 reshape.25
  71.6 0.0 copy-start.4
  71.6 0.0 copy-start.3
  71.6 2.5 %copy.40 = f32[1,4,96,768]{3,2,1,0:T(8,128)} copy(f32[1,4,96,768]{3,2,1,0:T(8,128)} %bitcast.27) | data formatting | bytes 2359296
  74.1 0.0 copy-start.2
  74.1 2.5 %copy.41 = f32[1,96,3072]{2,1,0:T(8,128)} copy(f32[1,96,3072]{2,1,0:T(8,128)} %bitcast.26) | data formatting | bytes 2359296
  76.6 0.0 copy-done.4
  76.6 0.0 slice-start.2
  76.6 1.0 %copy.42 = f32[1,384,768]{2,1,0:T(8,128)} copy(f32[1,384,768]{2,1,0:T(8,128)S(1)} %bitcast.25) | data formatting | bytes 2359296
  77.6 0.0 copy-done.3
  77.6 0.0 copy-start.5
  77.6 1.0 %copy.43 = f32[4,96,768]{2,1,0:T(8,128)} copy(f32[4,96,768]{2,1,0:T(8,128)S(1)} %copy-done.3) | data formatting | bytes 2359296
  78.6 0.0 copy-done.2
  78.6 0.0 copy-start
  78.6 1.0 %copy.44 = f32[96,3072]{1,0:T(8,128)} copy(f32[96,3072]{1,0:T(8,128)S(1)} %copy-done.2) | data formatting | bytes 2359296
  79.6 0.0 copy-done.1
  79.6 1.0 %copy.45 = f32[384,768]{1,0:T(8,128)} copy(f32[384,768]{1,0:T(8,128)S(1)} %copy-done.1) | data formatting | bytes 2359296
  80.7 0.0 copy-done.5
  80.7 0.0 slice-start.3
  80.7 0.6 copy.46
  81.2 0.7 copy-done
  81.9 0.0 slice-start
  81.9 2.4 %copy.47 = bf16[4,768,768]{2,1,0:T(8,128)(2,1)} copy(bf16[4,768,768]{2,1,0:T(8,128)(2,1)S(1)} %copy-done) | data formatting | bytes 9437184
  84.3 0.0 slice-done.2
  84.3 0.0 slice-done.3
  84.3 0.0 slice-start.1
  84.3 2.4 %copy.48 = bf16[768,3072]{1,0:T(8,128)(2,1)} copy(bf16[768,3072]{1,0:T(8,128)(2,1)S(1)} %bitcast.18) | data formatting | bytes 9437184
  86.7 0.4 slice-done
  87.2 0.6 slice-done.1
  87.8 2.2 %copy.49 = bf16[3072,768]{1,0:T(8,128)(2,1)} copy(bf16[3072,768]{1,0:T(8,128)(2,1)S(1)} %bitcast.16) | data formatting | bytes 9437184
  (4 shorter events, 0.0 us)
Async XLA Ops:
  71.6 5.0 %copy-start.4 = (f32[384,768]{1,0:T(8,128)S(1)}, f32[384,768]{1,0:T(8,128)}, u32[]{:S(2)}) copy-start(f32[384,768]{1,0:T(8,128)} %get-tuple-element.24) | copy-start | bytes 3538948
  71.6 6.0 %copy-start.3 = (f32[4,96,768]{2,1,0:T(8,128)S(1)}, f32[4,96,768]{2,1,0:T(8,128)}, u32[]{:S(2)}) copy-start(f32[4,96,768]{2,1,0:T(8,128)} %get-tuple-element.47) | copy-start | bytes 3538948
  74.1 4.6 %copy-start.2 = (f32[96,3072]{1,0:T(8,128)S(1)}, f32[96,3072]{1,0:T(8,128)}, u32[]{:S(2)}) copy-start(f32[96,3072]{1,0:T(8,128)} %get-tuple-element.48) | copy-start | bytes 3538948
  74.1 5.6 %copy-start.1 = (f32[384,768]{1,0:T(8,128)S(1)}, f32[384,768]{1,0:T(8,128)}, u32[]{:S(2)}) copy-start(f32[384,768]{1,0:T(8,128)} %get-tuple-element.49) | copy-start | bytes 3538948
  76.6 7.7 %slice-start.2 = ((s8[4718592]{0:T(1024)(128)(4,1)}), s8[4194304]{0:T(1024)(128)(4,1)S(1)}, s32[]{:S(2)}) async-start(s8[4718592]{0:T(1024)(128)(4,1)} %bitcast.17), calls=%async_computation.2 | async-start | bytes 8388608
  77.6 3.1 %copy-start.5 = (f32[4,96]{1,0:T(4,128)S(1)}, f32[4,96]{1,0:T(4,128)}, u32[]{:S(2)}) copy-start(f32[4,96]{1,0:T(4,128)} %get-tuple-element.50) | copy-start | bytes 4612
  78.6 3.3 %copy-start = (bf16[4,768,768]{2,1,0:T(8,128)(2,1)S(1)}, bf16[4,768,768]{2,1,0:T(8,128)(2,1)}, u32[]{:S(2)}) copy-start(bf16[4,768,768]{2,1,0:T(8,128)(2,1)} %get-tuple-element.51) | copy-start | bytes 14155780
  80.7 3.6 %slice-start.3 = ((s8[4718592]{0:T(1024)(128)(4,1)}), s8[524288]{0:T(1024)(128)(4,1)S(1)}, s32[]{:S(2)}) async-start(s8[4718592]{0:T(1024)(128)(4,1)} %bitcast.17), calls=%async_computation.3 | async-start | bytes 1048576
  81.9 5.3 %slice-start = ((s8[4718592]{0:T(1024)(128)(4,1)}), s8[4194304]{0:T(1024)(128)(4,1)S(1)}, s32[]{:S(2)}) async-start(s8[4718592]{0:T(1024)(128)(4,1)} %bitcast.15), calls=%async_computation | async-start | bytes 8388608
  84.3 3.5 %slice-start.1 = ((s8[4718592]{0:T(1024)(128)(4,1)}), s8[524288]{0:T(1024)(128)(4,1)S(1)}, s32[]{:S(2)}) async-start(s8[4718592]{0:T(1024)(128)(4,1)} %bitcast.15), calls=%async_computation.1 | async-start | bytes 1048576
